TPU v7x, 128 devices: a whole 4x4x4 slice. The times are simulated.
128 devices in a mesh: row: 8 (over z, core), col: 16 (over x, y).
Axes of the slice: x: 4, y: 4, z: 4, core: 2. Of those that a mesh axis runs over, the one named last changes fastest.
Arguments:
- features: bfloat16 [262144, 512], P(('row', 'col')), may hold values from -6 to 6
- history: bfloat16 [262144, 512], P(('row', 'col')), may hold values from -6 to 6
- cotangent: bfloat16 [262144, 512], P(('row', 'col')), may hold values from -0.03125 to 0.03125
- adjacency: bfloat16 [262144, 8, 128], P(('row', 'col')), as said below
- tile_source: int32 [2048, 8], P(('row', 'col')), may hold values from 0 to 39, as said below
- col_sends: int32 [128, 16, 1], P(('row', 'col')), may hold values from 0 to 15, as said below
- col_counts: int32 [128, 16], P(('row', 'col')), may hold values from 0 to 1, as said below
- row_sends: int32 [128, 8, 1], P(('row', 'col')), may hold values from 0 to 15, as said below
- row_counts: int32 [128, 8], P(('row', 'col')), may hold values from 0 to 1, as said below
- first_self: bfloat16 [512, 512], replicated, may hold values from -0.25 to 0.25
- first_neigh: bfloat16 [512, 512], replicated, may hold values from -1 to 1
- second_self: bfloat16 [512, 512], replicated, may hold values from -0.25 to 0.25
- second_neigh: bfloat16 [512, 512], replicated, may hold values from -1 to 1
Outputs:
- embeddings: bfloat16 [262144, 512], P(('row', 'col'))
- fresh_halo: bfloat16 [393216, 512], P(('row', 'col'))
- grad_first_self: float32 [512, 512], replicated
- grad_first_neigh: float32 [512, 512], replicated
- grad_second_self: float32 [512, 512], replicated
- grad_second_neigh: float32 [512, 512], replicated
Inputs may be any that keep to these rules, and one draw needn't show every extreme that they name: col_counts[p, d] is 0 where d is p's own grid column. In every draw one partition receives 1 block from every other partition of its grid row and of its grid column. row_counts[p, d] is 0 where d is p's own grid row. `col_sends`: local block numbers of the sending partition. `row_sends`: local block numbers of the sending partition. `tile_source`: below 16: a local block; from 16 on: halo slot number plus 16. Only used halo slots are named. `adjacency`: Nonnegative; entry [n, 0, n mod 128] is positive for every node n.
All inputs are finite; a program needn't handle non-finite values.
Results may differ from a plain program's by a relative error of at most 0.0054.
Values may be sent and summed in bfloat16 or wider, within the bound.
A program may use at most 192 MiB of HBM per device.

v0:
```python
import jax
import jax.numpy as jnp
from jax import lax
from jax.sharding import PartitionSpec as P


def activation(inputs):
    return jax.nn.gelu(inputs, approximate=True)


def pack_blocks(blocks, slot_ids, live_counts):
    chosen = jnp.take(blocks, slot_ids.reshape(-1), axis=0)
    chosen = chosen.reshape(slot_ids.shape + blocks.shape[1:])
    usable = jnp.arange(slot_ids.shape[1])[None, :] < live_counts[:, None]
    return jnp.where(usable[:, :, None, None], chosen, jnp.zeros((), blocks.dtype))


def join_halo(from_col, from_row):
    block_rows = from_col.shape[2]
    feature_width = from_col.shape[3]
    return jnp.concatenate(
        [
            from_col.reshape(-1, block_rows, feature_width),
            from_row.reshape(-1, block_rows, feature_width),
        ],
        axis=0,
    )


def aggregate(own_part, halo_part, adjacency, tile_source):
    block_total, tile_count = tile_source.shape
    block_rows = own_part.shape[1]
    feature_width = own_part.shape[2]
    sources = jnp.concatenate([own_part, halo_part], axis=0)
    gathered = jnp.take(sources, tile_source.reshape(-1), axis=0).reshape(
        block_total, tile_count, block_rows, feature_width
    )
    adj_tiles = adjacency.reshape(block_total, block_rows, tile_count, block_rows)
    summed = jnp.einsum("irtc,itcw->irw", adj_tiles, gathered, preferred_element_type=jnp.float32)
    return summed.reshape(block_total * block_rows, feature_width)


def body(
    features,
    history,
    cotangent,
    adjacency,
    tile_source,
    col_sends,
    col_counts,
    row_sends,
    row_counts,
    first_self,
    first_neigh,
    second_self,
    second_neigh,
):
    own_rows, tile_count, block_rows = adjacency.shape
    own_blocks = own_rows // block_rows
    hidden_width = history.shape[1]
    col_slots = col_sends[0]
    col_live = col_counts[0]
    row_slots = row_sends[0]
    row_live = row_counts[0]
    feat_blocks = features.reshape(own_blocks, block_rows, -1)
    hist_blocks = history.reshape(own_blocks, block_rows, -1)
    degree = jnp.sum(adjacency, axis=(1, 2), dtype=jnp.float32)[:, None]
    col_feat = lax.all_to_all(
        pack_blocks(feat_blocks, col_slots, col_live),
        "col",
        split_axis=0,
        concat_axis=0,
        tiled=True,
    )
    row_feat = lax.all_to_all(
        pack_blocks(feat_blocks, row_slots, row_live),
        "row",
        split_axis=0,
        concat_axis=0,
        tiled=True,
    )
    feat_halo = join_halo(col_feat, row_feat)
    first_mean = (aggregate(feat_blocks, feat_halo, adjacency, tile_source) / degree).astype(
        jnp.bfloat16
    )
    first_pre = jnp.dot(features, first_self, preferred_element_type=jnp.float32) + jnp.dot(
        first_mean, first_neigh, preferred_element_type=jnp.float32
    )
    first_hidden = activation(first_pre).astype(jnp.bfloat16)
    hidden_blocks = first_hidden.reshape(own_blocks, block_rows, -1)
    col_hist, col_fresh = (
        lax.all_to_all(
            pack_blocks(hist_blocks, col_slots, col_live),
            "col",
            split_axis=0,
            concat_axis=0,
            tiled=True,
        ),
        lax.all_to_all(
            pack_blocks(hidden_blocks, col_slots, col_live),
            "col",
            split_axis=0,
            concat_axis=0,
            tiled=True,
        ),
    )
    row_hist, row_fresh = (
        lax.all_to_all(
            pack_blocks(hist_blocks, row_slots, row_live),
            "row",
            split_axis=0,
            concat_axis=0,
            tiled=True,
        ),
        lax.all_to_all(
            pack_blocks(hidden_blocks, row_slots, row_live),
            "row",
            split_axis=0,
            concat_axis=0,
            tiled=True,
        ),
    )
    hist_halo = join_halo(col_hist, row_hist)
    fresh_halo = join_halo(col_fresh, row_fresh).reshape(-1, hidden_width)
    second_mean = (aggregate(hidden_blocks, hist_halo, adjacency, tile_source) / degree).astype(
        jnp.bfloat16
    )
    embeddings = (
        jnp.dot(first_hidden, second_self, preferred_element_type=jnp.float32)
        + jnp.dot(second_mean, second_neigh, preferred_element_type=jnp.float32)
    ).astype(jnp.bfloat16)
    grad_second_self = jnp.einsum(
        "nf,nh->fh", first_hidden, cotangent, preferred_element_type=jnp.float32
    )
    grad_second_neigh = jnp.einsum(
        "nf,nh->fh", second_mean, cotangent, preferred_element_type=jnp.float32
    )
    back_self = jnp.dot(cotangent, second_self.T, preferred_element_type=jnp.float32)
    back_mean = (
        jnp.dot(cotangent, second_neigh.T, preferred_element_type=jnp.float32) / degree
    ).astype(jnp.bfloat16)
    adj_tiles = adjacency.reshape(own_blocks, block_rows, tile_count, block_rows)
    spread = jnp.einsum(
        "irtc,irw->itcw",
        adj_tiles,
        back_mean.reshape(own_blocks, block_rows, hidden_width),
        preferred_element_type=jnp.float32,
    )
    onehot = (
        tile_source[:, :, None] == jnp.arange(own_blocks, dtype=jnp.int32)[None, None, :]
    ).astype(jnp.float32)
    back_neigh = jnp.einsum(
        "itj,itcw->jcw", onehot, spread, precision=lax.Precision.HIGHEST
    ).reshape(own_rows, hidden_width)
    unused_value, pullback = jax.vjp(activation, first_pre)
    back_pre = pullback(back_self + back_neigh)[0].astype(jnp.bfloat16)
    grad_first_self = jnp.einsum(
        "nf,nh->fh", features, back_pre, preferred_element_type=jnp.float32
    )
    grad_first_neigh = jnp.einsum(
        "nf,nh->fh", first_mean, back_pre, preferred_element_type=jnp.float32
    )
    grad_first_self, grad_first_neigh, grad_second_self, grad_second_neigh = lax.psum(
        (grad_first_self, grad_first_neigh, grad_second_self, grad_second_neigh), ("row", "col")
    )
    return (
        embeddings,
        fresh_halo,
        grad_first_self,
        grad_first_neigh,
        grad_second_self,
        grad_second_neigh,
    )


def solution(mesh):
    placed = (
        P(("row", "col"), None),
        P(("row", "col"), None),
        P(("row", "col"), None),
        P(("row", "col"), None, None),
        P(("row", "col"), None),
        P(("row", "col"), None, None),
        P(("row", "col"), None),
        P(("row", "col"), None, None),
        P(("row", "col"), None),
        P(),
        P(),
        P(),
        P(),
    )
    return jax.shard_map(
        body,
        mesh=mesh,
        in_specs=placed,
        out_specs=(P(("row", "col"), None), P(("row", "col"), None), P(), P(), P(), P()),
        check_vma=False,
    )
```

profile of v0, /device:TPU:1, one launch (start us, length us, event | category | flops | bytes accessed | tf_op | source)
XLA Modules:
  0.0 479.4 jit_solution(8296875876857193495)
XLA Ops:
  9.3 2.2 gather_fusion.1
  11.5 1.2 fusion.19
  12.7 6.8 %all-to-all-start.1 = ((bf16[8,1,128,512]{3,2,1,0:T(8,128)(2,1)}), bf16[8,1,128,512]{3,2,1,0:T(8,128)(2,1)S(1)}, u32[]{:S(2)}, u32[]{:S(2)}) async-start(bf16[8,1,128,512]{3,2,1,0:T(8,128)(2,1)} %fusion.19), calls=%async_computation.1 | async-start | bytes 2097152 | tf_op jit(solution)/shard_map/all_to_all | solution.py:75
  19.6 3.6 gather_fusion
  23.2 3.4 fusion.16
  26.5 15.2 %convert_reduce_fusion = f32[2048]{0:T(1024)S(1)} fusion(bf16[2048,8,128]{2,1,0:T(8,128)(2,1)S(1)} %copy-done.1), kind=kLoop, calls=%fused_computation.11 | loop fusion | flops 4192256 | bytes 4202496 | tf_op jit(solution)/shard_map/reduce_sum | solution.py:67
  41.8 2.6 divide_convert_fusion
  44.4 7.3 %all-to-all-start = ((bf16[16,1,128,512]{3,2,1,0:T(8,128)(2,1)}), bf16[16,1,128,512]{3,2,1,0:T(8,128)(2,1)}, u32[]{:S(2)}, u32[]{:S(2)}) async-start(bf16[16,1,128,512]{3,2,1,0:T(8,128)(2,1)} %fusion.16), calls=%async_computation | async-start | bytes 4194304 | tf_op jit(solution)/shard_map/all_to_all | solution.py:68
  51.7 18.4 %convolution_bitcast_fusion = f32[16,8,128,512]{2,3,1,0:T(8,128)} fusion(bf16[16,128,512,1]{2,1,3,0:T(8,128)(2,1)} %bitcast.121, bf16[16,128,8,128]{3,2,1,0:T(8,128)(2,1)} %bitcast.110), kind=kOutput, calls=%fused_computation.10 | convolution fusion | flops 2147483648 | bytes 39845888 | tf_op jit(solution)/shard_map/irtc,irw->itcw/dot_general | solution.py:143
  71.0 33.9 %copy.39 = f32[16,8,128,512]{3,0,1,2:T(8,128)} copy(f32[16,8,128,512]{2,3,1,0:T(8,128)} %convolution_bitcast_fusion) | data formatting | bytes 67108864 | tf_op jit(solution)/shard_map/irtc,irw->itcw/dot_general | solution.py:143
  104.9 4.9 %fusion.23 = f32[2048,512]{1,0:T(8,128)} fusion(bf16[2048,512]{1,0:T(8,128)(2,1)} %param.19, bf16[512,512]{1,0:T(8,128)(2,1)} %param.28), kind=kOutput, calls=%fused_computation.66 | convolution fusion | flops 1073741824 | bytes 6815744 | tf_op jit(solution)/shard_map/dot_general | solution.py:86
  109.8 5.5 %pad_maximum_fusion = bf16[40,128,512]{2,1,0:T(8,128)(2,1)} fusion(bf16[8,128,512]{2,1,0:T(8,128)(2,1)} %bitcast.123, bf16[16,128,512]{2,1,0:T(8,128)(2,1)} %bitcast.4, bf16[16,128,512]{2,1,0:T(8,128)(2,1)} %bitcast.117), kind=kLoop, calls=%fused_computation.14 | loop fusion | flops 5242880 | bytes 10485760 | tf_op jit(solution)/shard_map/concatenate | solution.py:34
  115.3 10.9 %gather_fusion.2 = bf16[128,128,512]{2,1,0:T(8,128)(2,1)} fusion(bf16[40,128,512]{2,1,0:T(8,128)(2,1)} %pad_maximum_fusion, s32[1024]{0:T(1024)S(1)} %pad_clamp_fusion), kind=kCustom, calls=%fused_computation.2.clone | custom fusion | bytes 33554944 | tf_op jit(solution)/shard_map/jit(_take)/gather | solution.py:35
  126.2 14.5 %broadcast_select_fusion.1 = bf16[128,128,512]{2,1,0:T(8,128)(2,1)} fusion(bf16[128,128,512]{2,1,0:T(8,128)(2,1)} %gather_fusion.2, pred[128]{0:T(512)(128)(4,1)S(1)} %compare_and_fusion), kind=kLoop, calls=%fused_computation.9 | loop fusion | flops 8388608 | bytes 33554560 | tf_op jit(solution)/shard_map/jit(_take)/select_n | solution.py:35
  140.7 7.0 %fusion.10 = f32[16,512,128,1]{1,2,3,0:T(8,128)S(1)} fusion(bf16[16,8,128,512]{3,2,1,0:T(8,128)(2,1)} %bitcast.114, bf16[16,128,8,128]{3,2,1,0:T(8,128)(2,1)S(1)} %bitcast.111), kind=kOutput, calls=%fused_computation.33 | convolution fusion | flops 2147483648 | bytes 25165824 | tf_op jit(solution)/shard_map/irtc,itcw->irw/dot_general | solution.py:39
  148.1 1.8 copy-done.8
  150.0 4.9 %multiply_convert_fusion = (bf16[2048,512]{1,0:T(8,128)(2,1)}, f32[2048,512]{1,0:T(8,128)}) fusion(f32[2048,512]{1,0:T(8,128)S(1)} %copy-done.8, bf16[2048,512]{1,0:T(8,128)(2,1)S(1)} %fusion.8, bf16[512,512]{1,0:T(8,128)(2,1)S(1)} %copy-done.22), kind=kOutput, calls=%fused_computation.30 | convolution fusion | flops 1084227584 | bytes 13107200 | tf_op jit(solution)/shard_map/dot_general | solution.py:86
  154.9 3.2 gather_fusion.7
  158.1 2.8 fusion.17
  161.0 5.2 %all-to-all-start.3 = ((bf16[8,1,128,512]{3,2,1,0:T(8,128)(2,1)}), bf16[8,1,128,512]{3,2,1,0:T(8,128)(2,1)S(1)}, u32[]{:S(2)}, u32[]{:S(2)}) async-start(bf16[8,1,128,512]{3,2,1,0:T(8,128)(2,1)} %get-tuple-element.34), calls=%async_computation.3 | async-start | bytes 2097152 | tf_op jit(solution)/shard_map/all_to_all | solution.py:108
  166.2 21.8 %convolution_bitcast_fusion.1 = f32[16,128,512]{2,0,1:T(8,128)} fusion(f32[16,8,128,512]{3,0,1,2:T(8,128)} %copy.39, s32[16,8]{0,1:T(8,128)S(1)} %copy-done.18), kind=kOutput, calls=%fused_computation.38 | convolution fusion | flops 1610614784 | bytes 37749248 | tf_op jit(solution)/shard_map/itj,itcw->jcw/dot_general | solution.py:152
  188.0 2.1 gather_fusion.3
  190.1 6.6 %copy.40 = f32[16,128,512]{2,1,0:T(8,128)} copy(f32[16,128,512]{2,0,1:T(8,128)} %convolution_bitcast_fusion.1) | data formatting | bytes 8388608 | tf_op jit(solution)/shard_map/itj,itcw->jcw/dot_general | solution.py:152
  196.7 3.6 gather_fusion.6
  200.2 4.8 %fusion.14 = (bf16[16,1,128,512]{3,2,1,0:T(8,128)(2,1)}, bf16[16,1,128,512]{3,2,1,0:T(8,128)(2,1)}) fusion(bf16[16,128,512]{2,1,0:T(8,128)(2,1)} %gather_fusion.6, pred[16]{0:T(512)(128)(4,1)S(1)} %compare_and_fusion.2, pred[16]{0:T(512)(128)(4,1)S(1)} %compare_bitcast_fusion.1, bf16[16,128,512]{2,1,0:T(8,128)(2,1)} %gather_fusion.3), kind=kLoop, calls=%fused_computation.40 | loop fusion | flops 4194304 | bytes 8388640 | tf_op jit(solution)/shard_map/jit(_where)/select_n | solution.py:15
  205.1 7.3 %all-to-all-start.2 = ((bf16[16,1,128,512]{3,2,1,0:T(8,128)(2,1)}), bf16[16,1,128,512]{3,2,1,0:T(8,128)(2,1)}, u32[]{:S(2)}, u32[]{:S(2)}) async-start(bf16[16,1,128,512]{3,2,1,0:T(8,128)(2,1)} %get-tuple-element.32), calls=%async_computation.2 | async-start | bytes 4194304 | tf_op jit(solution)/shard_map/all_to_all | solution.py:92
  212.5 4.6 fusion.26
  217.1 5.2 %fusion.6 = bf16[2048,512]{1,0:T(8,128)(2,1)S(1)} fusion(f32[2048,512]{1,0:T(8,128)} %get-tuple-element.36, f32[16,128,512]{2,1,0:T(8,128)S(1)} %copy-done.10, bf16[2048,512]{1,0:T(8,128)(2,1)S(1)} %copy-done.20, bf16[512,512]{1,0:T(8,128)(2,1)S(1)} %copy-done.14), kind=kOutput, calls=%fused_computation.22 | convolution fusion | flops 1095761920 | bytes 13107200 | tf_op jit(solution)/shard_map/dot_general | solution.py:138
  222.3 2.2 fusion.25
  224.5 2.2 convolution_bitcast_fusion.2
  226.8 14.8 %all-to-all-done.2 = bf16[16,1,128,512]{3,2,1,0:T(8,128)(2,1)} async-done(((bf16[16,1,128,512]{3,2,1,0:T(8,128)(2,1)}), bf16[16,1,128,512]{3,2,1,0:T(8,128)(2,1)}, u32[]{:S(2)}, u32[]{:S(2)}) %all-to-all-start.2) | async-done | bytes 2097184 | tf_op jit(solution)/shard_map/all_to_all | solution.py:92
  241.5 7.2 %all-to-all-start.5 = ((bf16[8,1,128,512]{3,2,1,0:T(8,128)(2,1)}), bf16[8,1,128,512]{3,2,1,0:T(8,128)(2,1)}, u32[]{:S(2)}, u32[]{:S(2)}) async-start(bf16[8,1,128,512]{3,2,1,0:T(8,128)(2,1)} %get-tuple-element.33), calls=%async_computation.5 | async-start | bytes 2097152 | tf_op jit(solution)/shard_map/all_to_all | solution.py:115
  248.7 5.1 %pad_maximum_fusion.1 = bf16[40,128,512]{2,1,0:T(8,128)(2,1)} fusion(bf16[8,128,512]{2,1,0:T(8,128)(2,1)S(1)} %bitcast.122, bf16[16,128,512]{2,1,0:T(8,128)(2,1)} %bitcast.20, bf16[16,128,512]{2,1,0:T(8,128)(2,1)} %bitcast.120), kind=kLoop, calls=%fused_computation.15 | loop fusion | flops 5242880 | bytes 10485760 | tf_op jit(solution)/shard_map/concatenate | solution.py:34
  253.9 10.9 %gather_fusion.5 = bf16[128,128,512]{2,1,0:T(8,128)(2,1)} fusion(bf16[40,128,512]{2,1,0:T(8,128)(2,1)} %pad_maximum_fusion.1, s32[1024]{0:T(1024)S(1)} %pad_clamp_fusion), kind=kCustom, calls=%fused_computation.7.clone | custom fusion | bytes 33554944 | tf_op jit(solution)/shard_map/jit(_take)/gather | solution.py:35
  264.7 14.4 %broadcast_select_fusion = bf16[128,128,512]{2,1,0:T(8,128)(2,1)} fusion(bf16[128,128,512]{2,1,0:T(8,128)(2,1)} %gather_fusion.5, pred[128]{0:T(512)(128)(4,1)S(1)} %compare_and_fusion), kind=kLoop, calls=%fused_computation.8 | loop fusion | flops 8388608 | bytes 33554560 | tf_op jit(solution)/shard_map/jit(_take)/select_n | solution.py:35
  279.2 9.1 %fusion.12 = f32[16,512,128,1]{1,2,3,0:T(8,128)} fusion(bf16[16,8,128,512]{3,2,1,0:T(8,128)(2,1)} %bitcast.113, bf16[16,128,8,128]{3,2,1,0:T(8,128)(2,1)S(1)} %bitcast.112), kind=kOutput, calls=%fused_computation.35 | convolution fusion | flops 2147483648 | bytes 25165824 | tf_op jit(solution)/shard_map/irtc,itcw->irw/dot_general | solution.py:39
  288.3 4.4 all-to-all-start.4
  292.8 2.7 fusion.7
  295.5 1.4 copy-done.6
  296.9 2.2 fusion.27
  299.2 4.9 %fusion.24 = f32[2048,512]{1,0:T(8,128)} fusion(bf16[2048,512]{1,0:T(8,128)(2,1)} %get-tuple-element.35, bf16[512,512]{1,0:T(8,128)(2,1)S(1)} %copy-done.15), kind=kOutput, calls=%fused_computation.67 | convolution fusion | flops 1073741824 | bytes 6815744 | tf_op jit(solution)/shard_map/dot_general | solution.py:129
  304.1 18.0 %all-to-all-done.4 = bf16[16,1,128,512]{3,2,1,0:T(8,128)(2,1)} async-done(((bf16[16,1,128,512]{3,2,1,0:T(8,128)(2,1)}), bf16[16,1,128,512]{3,2,1,0:T(8,128)(2,1)}, u32[]{:S(2)}, u32[]{:S(2)}) %all-to-all-start.4) | async-done | bytes 2097184 | tf_op jit(solution)/shard_map/all_to_all | solution.py:99
  322.0 4.0 pad_maximum_fusion.2
  327.1 2.7 add_convert_fusion
  329.7 134.5 %all-reduce.3.cloned.1.call-done = (f32[512,512]{0,1:T(8,128)}, f32[512,512]{1,0:T(8,128)}, f32[512,512]{1,0:T(8,128)}, f32[512,512]{1,0:T(8,128)}) async-done(((f32[512,512]{0,1:T(8,128)}, f32[512,512]{1,0:T(8,128)}, f32[512,512]{1,0:T(8,128)}, f32[512,512]{1,0:T(8,128)}), (f32[512,512]{0,1:T(8,128)}, f32[512,512]{1,0:T(8,128)}, f32[512,512]{1,0:T(8,128)}, ...) | async-done | bytes 4194320 | tf_op jit(solution)/shard_map/psum | solution.py:163
  464.2 2.6 copy.41
  466.8 2.3 copy.58
  469.1 2.3 copy.59
  (70 shorter events, 5.6 us)
Async XLA Ops:
  7.2 63.2 %copy-start = (bf16[2048,512]{1,0:T(8,128)(2,1)S(1)}, bf16[2048,512]{1,0:T(8,128)(2,1)}, u32[]{:S(2)}) copy-start(bf16[2048,512]{1,0:T(8,128)(2,1)} %param.20) | copy-start | bytes 6291460
  7.2 12.3 %copy-start.23 = (s32[1,16,1]{1,2,0:T(1,128)S(1)}, s32[1,16,1]{1,2,0:T(1,128)}, u32[]{:S(2)}) copy-start(s32[1,16,1]{1,2,0:T(1,128)} %param.24) | copy-start | bytes 196
  7.2 12.4 %copy-start.24 = (s32[1,16]{1,0:T(1,128)S(1)}, s32[1,16]{1,0:T(1,128)}, u32[]{:S(2)}) copy-start(s32[1,16]{1,0:T(1,128)} %param.25) | copy-start | bytes 196
  12.7 31.7 %all-to-all-start.1 = ((bf16[8,1,128,512]{3,2,1,0:T(8,128)(2,1)}), bf16[8,1,128,512]{3,2,1,0:T(8,128)(2,1)S(1)}, u32[]{:S(2)}, u32[]{:S(2)}) async-start(bf16[8,1,128,512]{3,2,1,0:T(8,128)(2,1)} %fusion.19), calls=%async_computation.1 | async-start | bytes 2097152 | tf_op jit(solution)/shard_map/all_to_all | solution.py:75
  23.2 3.4 copy-start.1
  23.2 18.6 %copy-start.16 = (bf16[512,512]{1,0:T(8,128)(2,1)S(1)}, bf16[512,512]{1,0:T(8,128)(2,1)}, u32[]{:S(2)}) copy-start(bf16[512,512]{1,0:T(8,128)(2,1)} %param.31) | copy-start | bytes 1572868
  23.2 18.6 %copy-start.19 = (bf16[2048,512]{1,0:T(8,128)(2,1)S(1)}, bf16[2048,512]{1,0:T(8,128)(2,1)}, u32[]{:S(2)}) copy-start(bf16[2048,512]{1,0:T(8,128)(2,1)} %param.21) | copy-start | bytes 6291460
  44.4 25.7 %copy-start.9 = (bf16[8,1,128,512]{3,2,1,0:T(8,128)(2,1)}, bf16[8,1,128,512]{3,2,1,0:T(8,128)(2,1)S(1)}, u32[]{:S(2)}) copy-start(bf16[8,1,128,512]{3,2,1,0:T(8,128)(2,1)S(1)} %all-to-all-done.1) | copy-start | bytes 3145732
  44.4 65.4 %all-to-all-start = ((bf16[16,1,128,512]{3,2,1,0:T(8,128)(2,1)}), bf16[16,1,128,512]{3,2,1,0:T(8,128)(2,1)}, u32[]{:S(2)}, u32[]{:S(2)}) async-start(bf16[16,1,128,512]{3,2,1,0:T(8,128)(2,1)} %fusion.16), calls=%async_computation | async-start | bytes 4194304 | tf_op jit(solution)/shard_map/all_to_all | solution.py:68
  51.7 18.4 %copy-start.18 = (s32[16,8]{0,1:T(8,128)S(1)}, s32[16,8]{0,1:T(8,128)}, u32[]{:S(2)}) copy-start(s32[16,8]{0,1:T(8,128)} %param.23) | copy-start | bytes 1540
  126.2 14.5 %copy-start.2 = (bf16[2048,8,128]{2,1,0:T(8,128)(2,1)S(1)}, bf16[2048,8,128]{2,1,0:T(8,128)(2,1)}, u32[]{:S(2)}) copy-start(bf16[2048,8,128]{2,1,0:T(8,128)(2,1)} %param.22) | copy-start | bytes 12582916
  147.7 2.2 copy-start.8
  147.7 2.3 copy-start.22
  150.0 4.9 %copy-start.11 = (bf16[2048,512]{1,0:T(8,128)(2,1)}, bf16[2048,512]{1,0:T(8,128)(2,1)S(1)}, u32[]{:S(2)}) copy-start(bf16[2048,512]{1,0:T(8,128)(2,1)S(1)} %fusion.8) | copy-start | bytes 6291460
  161.0 44.1 %all-to-all-start.3 = ((bf16[8,1,128,512]{3,2,1,0:T(8,128)(2,1)}), bf16[8,1,128,512]{3,2,1,0:T(8,128)(2,1)S(1)}, u32[]{:S(2)}, u32[]{:S(2)}) async-start(bf16[8,1,128,512]{3,2,1,0:T(8,128)(2,1)} %get-tuple-element.34), calls=%async_computation.3 | async-start | bytes 2097152 | tf_op jit(solution)/shard_map/all_to_all | solution.py:108
  205.1 36.5 %all-to-all-start.2 = ((bf16[16,1,128,512]{3,2,1,0:T(8,128)(2,1)}), bf16[16,1,128,512]{3,2,1,0:T(8,128)(2,1)}, u32[]{:S(2)}, u32[]{:S(2)}) async-start(bf16[16,1,128,512]{3,2,1,0:T(8,128)(2,1)} %get-tuple-element.32), calls=%async_computation.2 | async-start | bytes 4194304 | tf_op jit(solution)/shard_map/all_to_all | solution.py:92
  212.4 4.7 copy-start.10
  212.4 4.6 copy-start.14
  212.4 4.6 copy-start.20
  217.1 5.2 %copy-start.12 = (bf16[2048,512]{1,0:T(8,128)(2,1)S(1)}, bf16[2048,512]{1,0:T(8,128)(2,1)}, u32[]{:S(2)}) copy-start(bf16[2048,512]{1,0:T(8,128)(2,1)} %copy-done.11) | copy-start | bytes 6291460
  222.3 2.3 copy-start.4
  241.5 46.7 %all-to-all-start.5 = ((bf16[8,1,128,512]{3,2,1,0:T(8,128)(2,1)}), bf16[8,1,128,512]{3,2,1,0:T(8,128)(2,1)}, u32[]{:S(2)}, u32[]{:S(2)}) async-start(bf16[8,1,128,512]{3,2,1,0:T(8,128)(2,1)} %get-tuple-element.33), calls=%async_computation.5 | async-start | bytes 2097152 | tf_op jit(solution)/shard_map/all_to_all | solution.py:115
  264.7 14.5 %copy-start.3 = (bf16[2048,8,128]{2,1,0:T(8,128)(2,1)S(1)}, bf16[2048,8,128]{2,1,0:T(8,128)(2,1)}, u32[]{:S(2)}) copy-start(bf16[2048,8,128]{2,1,0:T(8,128)(2,1)} %param.22) | copy-start | bytes 12582916
  288.3 33.8 %all-to-all-start.4 = ((bf16[16,1,128,512]{3,2,1,0:T(8,128)(2,1)}), bf16[16,1,128,512]{3,2,1,0:T(8,128)(2,1)}, u32[]{:S(2)}, u32[]{:S(2)}) async-start(bf16[16,1,128,512]{3,2,1,0:T(8,128)(2,1)} %get-tuple-element.31), calls=%async_computation.4 | async-start | bytes 4194304 | tf_op jit(solution)/shard_map/all_to_all | solution.py:99
  292.7 171.5 %all-reduce.3.cloned.1.call-start = ((), (), s32[]{:S(2)}) async-start(), calls=%async_computation.6 | async-start | bytes 8388608 | tf_op jit(solution)/shard_map/psum | solution.py:163
  292.8 4.1 copy-start.21
  295.5 1.4 copy-start.6
  296.9 2.3 copy-start.15
  299.2 26.9 %copy-start.17 = (bf16[512,512]{1,0:T(8,128)(2,1)S(1)}, bf16[512,512]{1,0:T(8,128)(2,1)}, u32[]{:S(2)}) copy-start(bf16[512,512]{1,0:T(8,128)(2,1)} %param.31) | copy-start | bytes 1572868
  322.0 4.0 copy-start.5
  322.0 5.0 %copy-start.7 = (bf16[2048,512]{1,0:T(8,128)(2,1)S(1)}, bf16[2048,512]{1,0:T(8,128)(2,1)}, u32[]{:S(2)}) copy-start(bf16[2048,512]{1,0:T(8,128)(2,1)} %copy-done.6) | copy-start | bytes 6291460
  464.2 7.1 %copy-start.13 = (f32[512,512]{1,0:T(8,128)S(1)}, f32[512,512]{1,0:T(8,128)}, u32[]{:S(2)}) copy-start(f32[512,512]{1,0:T(8,128)} %get-tuple-element.42) | copy-start | bytes 3145732
Sparse Core Ops, SparseCore 0:
  299.7 164.5 all-reduce.2
where the time goes:
time: 486 us; the launch traced here: 479 us
  waiting for transfers between devices  167 us (34%)
  matrix products  92.9 us (19%)
  local copies, waits for them, and re-layouts  90.2 us (19%)
  other arithmetic  76.2 us (16%)
  starting transfers between devices  38.3 us (8%)
  between operations  14.6 us (3%)
    psum x1, waiting for transfers between devices, body(): lax.psum((grad_first_self, grad_first_neigh, grad_second_self, grad_secon...  134 us
    dot_general x1, local copies, waits for them, and re-layouts, body(): jnp.einsum('irtc,irw->itcw', adj_tiles, back_mean.reshape(own_blocks, blo...  33.9 us
    select_n x3, other arithmetic, aggregate(): jnp.take(sources, tile_source.reshape(-1), axis=0)  29 us
    dot_general x1, matrix products, body(): jnp.einsum('itj,itcw->jcw', onehot, spread, precision=lax.Precision.HIGHEST)  21.8 us
    gather x2, local copies, waits for them, and re-layouts, aggregate(): jnp.take(sources, tile_source.reshape(-1), axis=0)  21.8 us
    dot_general x1, matrix products, body(): jnp.einsum('irtc,irw->itcw', adj_tiles, back_mean.reshape(own_blocks, blo...  18.4 us
    all_to_all x1, waiting for transfers between devices, body(): lax.all_to_all(pack_blocks(hidden_blocks, col_slots, col_live), 'col', sp...  18 us
    dot_general x2, matrix products, aggregate(): jnp.einsum('irtc,itcw->irw', adj_tiles, gathered, preferred_element_type=...  16.1 us
  transfers between devices with their start and end apart: 7, of which 3 were waited for; matrix products, arithmetic and copies ran while one was open for 40% of the time, Pallas kernels for 0%

commit v1 on v0

v1 whole, which is shorter than its diff:
```python
import functools

import jax
import jax.numpy as jnp
from jax import lax
from jax.experimental import pallas as pl
from jax.experimental.pallas import tpu as pltpu
from jax.sharding import PartitionSpec as P

MESH = pl.DeviceIdType.MESH
BF = jnp.bfloat16
F32 = jnp.float32
BLK = 128
TPB = 8
NB = 16
W = 512
LOC = NB * BLK
GELU_C = 0.7978845608028654
GELU_A = 0.044715

COL_OFFS = [
    (2, 2), (3, 2), (2, 3), (1, 2), (2, 1), (3, 1), (1, 3), (3, 3), (1, 1),
    (0, 2), (2, 0), (0, 3), (3, 0), (0, 1), (1, 0),
]
ROW_OFFS = [(2, 1), (2, 0), (3, 1), (1, 1), (3, 0), (1, 0), (0, 1)]
N_OFF = len(COL_OFFS) + len(ROW_OFFS)
TURNS = []
for _n in range(len(COL_OFFS)):
    TURNS.append(("col", _n))
    if _n % 2 == 0 and _n // 2 < len(ROW_OFFS):
        TURNS.append(("row", _n // 2))
FRESH_CUTS = (0, 22, 22, 22)


def dot(a, b):
    return jnp.dot(a, b, preferred_element_type=F32)


def dot_nt(a, b):
    return lax.dot_general(a, b, (((1,), (1,)), ((), ())), preferred_element_type=F32)


def dot_tn(a, b):
    return lax.dot_general(a, b, (((0,), (0,)), ((), ())), preferred_element_type=F32)


def blk(i):
    return pl.ds(pl.multiple_of(i * BLK, BLK), BLK)


def rows(i, n):
    return pl.ds(pl.multiple_of(i, n), n)


def kernel(
    feat_h, hist_h, cot_h, adj_h, ts, cs, cc, rs, rc, w1s_h, w1n_h, w2s_h, w2n_h,
    emb_h, fresh_h, grad_h,
    tab1, tab2, feat_v, hid_v, hist_v, snd_a, snd_b, cot, adjr, adjd, scr, deg, wts, fm, bm, acc, bp, sm, strip,
    rv1, s2, rv2, s3, h3, rv3, gfin,
    ld_sem, out_sem, a_ss, a_rs, b_ss, b_rs, f_ss, f_rs, r_ss, r_rs,
):
    c = lax.axis_index("col")
    r = lax.axis_index("row")
    x, y, z, k = c // 4, c % 4, r // 2, r % 2

    loads = [
        pltpu.make_async_copy(src, dst, ld_sem.at[n])
        for n, (src, dst) in enumerate(
            [
                (feat_h, feat_v),
                (hist_h, hist_v),
                (adj_h, adjr),
                (cot_h, cot),
                (w2s_h, wts.at[2]),
                (w2n_h, wts.at[3]),
                (w1s_h, wts.at[0]),
                (w1n_h, wts.at[1]),
                (feat_h, tab1.at[pl.ds(0, LOC)]),
            ]
        )
    ]
    for one in loads:
        one.start()

    def col_of(n, sign=1):
        a, b = COL_OFFS[n]
        dx = (1 - k) * a + k * b
        dy = (1 - k) * b + k * a
        return ((x + 4 + sign * dx) % 4) * 4 + (y + 4 + sign * dy) % 4

    def row_of(n, sign=1):
        a, b = ROW_OFFS[n]
        return ((z + 4 + sign * a) % 4) * 2 + (k + b) % 2

    barrier = pltpu.get_barrier_semaphore()
    for n in range(len(COL_OFFS)):
        pl.semaphore_signal(barrier, 1, device_id={"col": col_of(n)}, device_id_type=MESH)
    for n in range(len(ROW_OFFS)):
        pl.semaphore_signal(barrier, 1, device_id={"row": row_of(n)}, device_id_type=MESH)
    pl.semaphore_wait(barrier, N_OFF)

    def exchange(own, snd, dst, base, ssem, rsem, masked, first, last):
        copies = []
        for turn in range(first, last):
            kind, n = TURNS[turn]
            if kind == "col":
                to = col_of(n)
                which, live = cs[0, to, 0], cc[0, to]
                slot, device = base + c, {"col": to}
            else:
                to = row_of(n)
                which, live = rs[0, to, 0], rc[0, to]
                slot, device = base + 16 + r, {"row": to}
            chosen = own[pl.ds(which * BLK, BLK), :]
            if masked:
                chosen = jnp.where(jnp.full(chosen.shape, live, jnp.int32) > 0, chosen.astype(F32), 0.0)
                chosen = chosen.astype(BF)
            snd[pl.ds(turn * BLK, BLK), :] = chosen
            one = pltpu.make_async_remote_copy(
                src_ref=snd.at[pl.ds(turn * BLK, BLK)],
                dst_ref=dst.at[blk(slot)],
                send_sem=ssem.at[turn],
                recv_sem=rsem.at[turn],
                device_id=device,
                device_id_type=MESH,
            )
            one.start()
            copies.append(one)
        return copies

    loads[0].wait()
    feat_copies = exchange(feat_v, snd_a, tab1, NB, a_ss, a_rs, False, 0, N_OFF)
    loads[1].wait()
    hist_copies = exchange(hist_v, snd_b, tab2, NB, b_ss, b_rs, False, 0, N_OFF)

    zero_block = jnp.zeros((BLK, W), BF)
    for table in (tab1, tab2):
        table[blk(NB + c), :] = zero_block
        table[blk(NB + 16 + r), :] = zero_block

    loads[2].wait()

    @pl.loop(0, NB)
    def _(i):
        scr[...] = adjr[rows(i * BLK * TPB, BLK * TPB), :].astype(F32)
        total = jnp.zeros((BLK, BLK), F32)
        for t in range(TPB):
            tile = scr[pl.ds(t, BLK, stride=TPB), :]
            adjd[blk(i), pl.ds(t * BLK, BLK)] = tile.astype(BF)
            total += tile
        deg[blk(i), :] = jnp.broadcast_to(jnp.sum(total, axis=1, keepdims=True), (BLK, BLK))

    def divide(v, at):
        d = deg[at, :]
        return v / jnp.concatenate([d] * (W // BLK), axis=1)

    for n in range(3, 9):
        loads[n].wait()

    @pl.loop(0, 8)
    def _(m):
        at = rows(m * 256, 256)
        up = cot[at, :]
        acc[m // 2, rows((m % 2) * 256, 256), :] = dot_nt(up, wts[2])
        bm[at, :] = divide(dot_nt(up, wts[3]), at).astype(BF)

    @pl.loop(0, 8)
    def _(jp):
        @pl.loop(0, NB)
        def _(i):
            for jj in range(2):
                strip_part = jnp.zeros((BLK, BLK), F32)
                for t in range(TPB):
                    source = jnp.full((BLK, BLK), ts[i, t], jnp.int32)
                    tile = adjd[blk(i), pl.ds(t * BLK, BLK)].astype(F32)
                    strip_part += jnp.where(source == jp * 2 + jj, tile, 0.0)
                strip[blk(i), pl.ds(jj * BLK, BLK)] = strip_part.astype(BF)

        at = rows((jp % 2) * 256, 256)
        acc[jp // 2, at, :] += dot_tn(strip[...], bm[...])

    def aggregate(table, out):
        @pl.loop(0, NB)
        def _(i):
            total = jnp.zeros((BLK, W), F32)
            for t in range(0, TPB, 2):
                pair = jnp.concatenate(
                    [table[pl.ds(ts[i, t + d] * BLK, BLK), :] for d in range(2)], axis=0
                )
                total += dot(adjd[blk(i), pl.ds(t * BLK, 2 * BLK)], pair)
            out[blk(i), :] = divide(total, blk(i)).astype(BF)

    for one in feat_copies:
        one.wait_recv()
    aggregate(tab1, fm)

    @pl.loop(0, 8)
    def _(m):
        at = rows(m * 256, 256)
        v = dot(feat_v[at, :], wts[0]) + dot(fm[at, :], wts[1])
        t = jnp.tanh(GELU_C * (v + GELU_A * (v * v * v)))
        half = 0.5 * (1.0 + t)
        hidden = (v * half).astype(BF)
        hid_v[at, :] = hidden
        tab2[at, :] = hidden
        slope = half + 0.5 * v * (1.0 - t * t) * (GELU_C * (1.0 + 3.0 * GELU_A * (v * v)))
        bp[at, :] = (acc[m // 2, rows((m % 2) * 256, 256), :] * slope).astype(BF)

    for one in feat_copies:
        one.wait_send()
    fresh_copies = []

    def send_fresh(part):
        fresh_copies.extend(
            exchange(hid_v, snd_a, fresh_h, 0, f_ss, f_rs, True, FRESH_CUTS[part], FRESH_CUTS[part + 1])
        )

    send_fresh(0)

    def grad_of(g, left, right):
        @pl.loop(0, 4)
        def _(q):
            at = rows(q * BLK, BLK)
            acc[g, at, :] = dot_tn(left[:, at], right[...])

    grad_of(0, feat_v, bp)
    grad_of(1, fm, bp)
    grad_of(2, hid_v, cot)

    sems = iter(range(64))

    def send(src, dst, device):
        n = next(sems)
        one = pltpu.make_async_remote_copy(
            src_ref=src, dst_ref=dst, send_sem=r_ss.at[n], recv_sem=r_rs.at[n],
            device_id=device, device_id_type=MESH,
        )
        one.start()
        return one

    other = z * 2 + 1 - k
    reduce_copies = []

    def core_send(g, n):
        part = pl.ds(g, n)
        one = send(acc.at[part, rows((1 - k) * 256, 256)], rv1.at[part], {"row": other})
        reduce_copies.append(one)
        return one

    def z_send(g, n, core_copy):
        core_copy.wait_recv()
        for p in range(g, g + n):
            at = rows(k * 256, 256)
            both = acc[p, at, :] + rv1[p]
            acc[p, at, :] = both
            s2[p] = both.astype(BF)
        part = pl.ds(g, n)
        copies = []
        for d in range(3):
            zt = (z + d + 1) % 4
            copies.append(
                send(s2.at[part, rows(zt * 64, 64)], rv2.at[d, part], {"row": zt * 2 + k})
            )
        reduce_copies.extend(copies)
        return copies

    core_a = core_send(0, 3)
    for one in hist_copies:
        one.wait_recv()
    z_a = z_send(0, 3, core_a)
    send_fresh(1)
    aggregate(tab2, sm)
    grad_of(3, sm, cot)
    core_b = core_send(3, 1)

    snd_b_done = [one.wait_send() for one in hist_copies]
    snd_b[pl.ds(0, BLK), :] = zero_block
    own_slots = [
        pltpu.make_async_copy(snd_b.at[pl.ds(0, BLK)], fresh_h.at[blk(c)], out_sem.at[0]),
        pltpu.make_async_copy(snd_b.at[pl.ds(0, BLK)], fresh_h.at[blk(16 + r)], out_sem.at[1]),
    ]
    for one in own_slots:
        one.start()

    z_b = z_send(3, 1, core_b)

    @pl.loop(0, 4)
    def _(m):
        at = rows(m * 512, 512)
        bm[at, :] = (dot(hid_v[at, :], wts[2]) + dot(sm[at, :], wts[3])).astype(BF)

    emb_copy = pltpu.make_async_copy(bm, emb_h, out_sem.at[2])
    emb_copy.start()

    for one in z_a + z_b:
        one.wait_recv()
    for p in range(4):
        total = acc[p, rows(k * 256 + z * 64, 64), :]
        for d in range(3):
            total = total + rv2[d, p].astype(F32)
        h3[p] = total
        s3[p] = total.astype(BF)

    def piece(to):
        return (slice(None), rows((to // 4) * 16, 16), rows((to % 4) * BLK, BLK))

    xy_copies = []
    for n in range(len(COL_OFFS)):
        to = col_of(n)
        xy_copies.append(send(s3.at[piece(to)], rv3.at[n], {"col": to}))
    reduce_copies.extend(xy_copies)
    send_fresh(2)
    mine = (slice(None), rows(x * 16, 16), rows(y * BLK, BLK))
    final = h3[mine]
    for one in xy_copies:
        one.wait_recv()
    for n in range(len(COL_OFFS)):
        final = final + rv3[n].astype(F32)
    here = (slice(None), rows(k * 256 + z * 64 + x * 16, 16), rows(y * BLK, BLK))
    gfin[here] = final.astype(BF)

    gather = [send(gfin.at[here], gfin.at[here], {"col": col_of(n)}) for n in range(len(COL_OFFS))]
    for one in gather:
        one.wait_recv()
    reduce_copies.extend(gather)
    strip_z = (slice(None), rows(k * 256 + z * 64, 64))
    gather = [send(gfin.at[strip_z], gfin.at[strip_z], {"row": ((z + d + 1) % 4) * 2 + k}) for d in range(3)]
    for one in gather:
        one.wait_recv()
    reduce_copies.extend(gather)
    strip_k = (slice(None), rows(k * 256, 256))
    one = send(gfin.at[strip_k], gfin.at[strip_k], {"row": other})
    one.wait_recv()
    reduce_copies.append(one)
    grad_copy = pltpu.make_async_copy(gfin, grad_h, out_sem.at[3])
    grad_copy.start()

    for one in fresh_copies:
        one.wait_recv()
    for one in fresh_copies + reduce_copies:
        one.wait_send()
    for one in own_slots:
        one.wait()
    emb_copy.wait()
    grad_copy.wait()


def body(
    features, history, cotangent, adjacency, tile_source, col_sends, col_counts, row_sends, row_counts,
    first_self, first_neigh, second_self, second_neigh,
):
    anyspace = pl.BlockSpec(memory_space=pl.ANY)
    smem = pl.BlockSpec(memory_space=pltpu.SMEM)
    vm = pltpu.VMEM
    dma = pltpu.SemaphoreType.DMA
    emb, fresh, grads = pl.pallas_call(
        kernel,
        out_shape=(
            jax.ShapeDtypeStruct((LOC, W), BF),
            jax.ShapeDtypeStruct((24 * BLK, W), BF),
            jax.ShapeDtypeStruct((4, W, W), BF),
        ),
        in_specs=[anyspace] * 4 + [smem] * 5 + [anyspace] * 4,
        out_specs=(anyspace,) * 3,
        scratch_shapes=[
            vm((40 * BLK, W), BF),
            vm((40 * BLK, W), BF),
            vm((LOC, W), BF),
            vm((LOC, W), BF),
            vm((LOC, W), BF),
            vm((N_OFF * BLK, W), BF),
            vm((N_OFF * BLK, W), BF),
            vm((LOC, W), BF),
            vm((LOC * TPB, BLK), BF),
            vm((LOC, TPB * BLK), BF),
            vm((BLK * TPB, BLK), F32),
            vm((LOC, BLK), F32),
            vm((4, W, W), BF),
            vm((LOC, W), BF),
            vm((LOC, W), BF),
            vm((4, W, W), F32),
            vm((LOC, W), BF),
            vm((LOC, W), BF),
            vm((LOC, 2 * BLK), BF),
            vm((4, 256, W), F32),
            vm((4, 256, W), BF),
            vm((3, 4, 64, W), BF),
            vm((4, 64, W), BF),
            vm((4, 64, W), F32),
            vm((15, 4, 16, BLK), BF),
            vm((4, W, W), BF),
            dma((9,)), dma((4,)),
            dma((N_OFF,)), dma((N_OFF,)), dma((N_OFF,)), dma((N_OFF,)), dma((N_OFF,)), dma((N_OFF,)),
            dma((42,)), dma((42,)),
        ],
        compiler_params=pltpu.CompilerParams(
            collective_id=0, has_side_effects=True, vmem_limit_bytes=61 * 2**20
        ),
        cost_estimate=pl.CostEstimate(flops=18 * 10**9, bytes_accessed=24 * 2**20, transcendentals=2**20),
    )(
        features, history, cotangent, adjacency.reshape(LOC * TPB, BLK), tile_source,
        col_sends, col_counts, row_sends, row_counts,
        first_self, first_neigh, second_self, second_neigh,
    )
    return emb, fresh, *(grads[n].astype(F32) for n in range(4))


def solution(mesh):
    nodes = P(("row", "col"), None)
    cube = P(("row", "col"), None, None)
    placed = (nodes, nodes, nodes, cube, nodes, cube, nodes, cube, nodes, P(), P(), P(), P())
    return jax.shard_map(
        body, mesh=mesh, in_specs=placed,
        out_specs=(nodes, nodes, P(), P(), P(), P()), check_vma=False,
    )
```

time: 486 us -> 125 us (0.26); the launches traced: 479 us -> 125 us
  waiting for transfers between devices: 167 us -> 0 us
  Pallas kernels: 0 us -> 112 us
  matrix products: 92.9 us -> 0 us
  local copies, waits for them, and re-layouts: 90.2 us -> 8.32 us
  other arithmetic: 76.2 us -> 3.9 us
  starting transfers between devices: 38.3 us -> 0 us
  between operations: 14.6 us -> 0.65 us
    psum x1 -> x0, waiting for transfers between devices: 134 us -> none  [body(): lax.psum((grad_first_self, grad_first_neigh, grad_second_self, grad_secon...]
    pallas_call x0 -> x1, Pallas kernels: none -> 112 us  [body(): pl.pallas_call(kernel, out_shape=(jax.ShapeDtypeStruct((LOC, W), BF), jax...]
    dot_general x14 -> x0, matrix products: 92.9 us -> none  [the longest x1 21.8 us: body(): jnp.einsum('itj,itcw->jcw', onehot, spread, precision=lax.Precision.HIGHEST)]
    select_n x9 -> x0, other arithmetic: 41.8 us -> none  [the longest x3 29 us: aggregate(): jnp.take(sources, tile_source.reshape(-1), axis=0)]
    dot_general x2 -> x0, local copies, waits for them, and re-layouts: 40.5 us -> none  [the longest x1 33.9 us: body(): jnp.einsum('irtc,irw->itcw', adj_tiles, back_mean.reshape(own_blocks, blo...]
    all_to_all x6 -> x0, starting transfers between devices: 38.3 us -> none  [the longest x1 7.34 us: body(): lax.all_to_all(pack_blocks(hist_blocks, col_slots, col_live), 'col', spli...]
    gather x8 -> x0, local copies, waits for them, and re-layouts: 37 us -> none  [the longest x2 21.8 us: aggregate(): jnp.take(sources, tile_source.reshape(-1), axis=0)]
    all_to_all x6 -> x0, waiting for transfers between devices: 32.7 us -> none  [the longest x1 18 us: body(): lax.all_to_all(pack_blocks(hidden_blocks, col_slots, col_live), 'col', sp...]
  transfers between devices with their start and end apart: 7 -> 0, of which waited for: 3 -> 0; matrix products, arithmetic and copies ran while one was open for 40% -> 0% of each run, Pallas kernels for 0% -> 0%
where the time goes in v1:
time: 125 us
  Pallas kernels  112 us (90%)
  local copies, waits for them, and re-layouts  8.32 us (7%)
  other arithmetic  3.9 us (3%)
    pallas_call x1, Pallas kernels, body(): pl.pallas_call(kernel, out_shape=(jax.ShapeDtypeStruct((LOC, W), BF), jax...  112 us
    unnamed x9, local copies, waits for them, and re-layouts  8.32 us
    convert_element_type x1, other arithmetic, body(): return (emb, fresh, *(grads[n].astype(F32) for n in range(4)))  3.9 us

profile of v1, /device:TPU:1, one launch (start us, length us, event | category | flops | bytes accessed | tf_op | source)
XLA Modules:
  0.0 124.8 jit_solution(14063295958914427549)
XLA Ops:
  0.6 1.3 %copy.21.rs = s32[1,8,1]{2,1,0:T(8,128)} copy(s32[1,8,1]{1,2,0:T(1,128)} %param.20) | data formatting | bytes 64 | tf_op args[7]
  2.0 1.4 %copy.19.ts = s32[16,8]{1,0:T(8,128)} copy(s32[16,8]{0,1:T(8,128)} %param.17) | data formatting | bytes 1024 | tf_op args[4]
  3.3 1.3 %copy.20.cs = s32[1,16,1]{2,1,0:T(8,128)} copy(s32[1,16,1]{1,2,0:T(1,128)} %param.18) | data formatting | bytes 128 | tf_op args[5]
  4.6 112.0 %shard_map.172 = (bf16[2048,512]{1,0:T(8,128)(2,1)}, bf16[3072,512]{1,0:T(8,128)(2,1)}, bf16[4,512,512]{2,1,0:T(8,128)(2,1)}) custom-call(bf16[2048,512]{1,0:T(8,128)(2,1)} %feat_h.1, bf16[2048,512]{1,0:T(8,128)(2,1)} %hist_h.1, bf16[2048,512]{1,0:T(8,128)(2,1)} %cot_h.1, bf16[16384,128]{1,0:T(8,128)(2,1)} %bitcast.13, s32[16,8]{1,0:T(8,128)} %copy.19.ts, ...), custom_call_target="tpu_custom_call" | custom-call | flops 17999998976 | bytes 25165824 | tf_op jit(solution)/shard_map/pallas_call | solution.py:356
  116.6 0.0 copy-start.1
  116.6 3.9 %bitcast_convert_fusion = (f32[512,512]{1,0:T(8,128)}, f32[512,512]{1,0:T(8,128)}, f32[512,512]{1,0:T(8,128)}, f32[512,512]{1,0:T(8,128)}) fusion(bf16[4,512,512]{2,1,0:T(8,128)(2,1)} %get-tuple-element.11), kind=kLoop, calls=%fused_computation | loop fusion | flops 1048576 | bytes 6291456 | tf_op jit(solution)/shard_map/convert_element_type | solution.py:405
  120.5 0.0 copy-done.1
  120.5 0.0 copy-start
  120.5 1.3 %copy.24 = bf16[2048,512]{1,0:T(8,128)(2,1)} copy(bf16[2048,512]{1,0:T(8,128)(2,1)S(1)} %copy-done.1) | data formatting | bytes 4194304
  121.8 1.3 %copy-done = bf16[3072,512]{1,0:T(8,128)(2,1)S(1)} copy-done((bf16[3072,512]{1,0:T(8,128)(2,1)S(1)}, bf16[3072,512]{1,0:T(8,128)(2,1)}, u32[]{:S(2)}) %copy-start) | copy-done | bytes 3145752
  123.2 1.7 %copy.25 = bf16[3072,512]{1,0:T(8,128)(2,1)} copy(bf16[3072,512]{1,0:T(8,128)(2,1)S(1)} %copy-done) | data formatting | bytes 6291456
Async XLA Ops:
  116.6 3.9 %copy-start.1 = (bf16[2048,512]{1,0:T(8,128)(2,1)S(1)}, bf16[2048,512]{1,0:T(8,128)(2,1)}, u32[]{:S(2)}) copy-start(bf16[2048,512]{1,0:T(8,128)(2,1)} %get-tuple-element.22) | copy-start | bytes 6291460
  120.5 2.6 %copy-start = (bf16[3072,512]{1,0:T(8,128)(2,1)S(1)}, bf16[3072,512]{1,0:T(8,128)(2,1)}, u32[]{:S(2)}) copy-start(bf16[3072,512]{1,0:T(8,128)(2,1)} %get-tuple-element.23) | copy-start | bytes 9437188

commit v2 on v1

--- a/solution.py
+++ b/solution.py
@@ -15,6 +15,8 @@
 NB = 16
 W = 512
 LOC = NB * BLK
+RING = 4
+ROWS_EARLY = 4
 GELU_C = 0.7978845608028654
 GELU_A = 0.044715
 
@@ -29,7 +31,7 @@
     TURNS.append(("col", _n))
     if _n % 2 == 0 and _n // 2 < len(ROW_OFFS):
         TURNS.append(("row", _n // 2))
-FRESH_CUTS = (0, 22, 22, 22)
+FRESH_CUTS = (0, 5, 8, 11, 13, 15)
 
 
 def dot(a, b):
@@ -55,10 +57,11 @@
 def kernel(
     feat_h, hist_h, cot_h, adj_h, ts, cs, cc, rs, rc, w1s_h, w1n_h, w2s_h, w2n_h,
     emb_h, fresh_h, grad_h,
-    tab1, tab2, feat_v, hid_v, hist_v, snd_a, snd_b, cot, adjr, adjd, scr, deg, wts, fm, bm, acc, bp, sm, strip,
-    rv1, s2, rv2, s3, h3, rv3, gfin,
-    ld_sem, out_sem, a_ss, a_rs, b_ss, b_rs, f_ss, f_rs, r_ss, r_rs,
+    tab1, tab2, feat_v, hid_v, hist_v, snd_a, snd_b, cot, adjr, adjd, scr, deg, wts, fm, bm, acc, strip,
+    rv1, s2, rv2, s3, h3, rv3, g3, gfin,
+    ld_sem, adj_sem, out_sem, a_ss, a_rs, b_ss, b_rs, f_ss, f_rs, r_ss, r_rs,
 ):
+    bp, sm = hist_v, fm
     c = lax.axis_index("col")
     r = lax.axis_index("row")
     x, y, z, k = c // 4, c % 4, r // 2, r % 2
@@ -69,7 +72,6 @@
             [
                 (feat_h, feat_v),
                 (hist_h, hist_v),
-                (adj_h, adjr),
                 (cot_h, cot),
                 (w2s_h, wts.at[2]),
                 (w2n_h, wts.at[3]),
@@ -99,17 +101,17 @@
         pl.semaphore_signal(barrier, 1, device_id={"row": row_of(n)}, device_id_type=MESH)
     pl.semaphore_wait(barrier, N_OFF)
 
-    def exchange(own, snd, dst, base, ssem, rsem, masked, first, last):
+    def exchange(own, snd, dst, base, ssem, rsem, masked, turns):
         copies = []
-        for turn in range(first, last):
-            kind, n = TURNS[turn]
+        for kind, n in turns:
+            turn = n if kind == "col" else len(COL_OFFS) + n
             if kind == "col":
                 to = col_of(n)
-                which, live = cs[0, to, 0], cc[0, to]
+                which, live = cs[0, to], cc[0, to]
                 slot, device = base + c, {"col": to}
             else:
                 to = row_of(n)
-                which, live = rs[0, to, 0], rc[0, to]
+                which, live = rs[0, to], rc[0, to]
                 slot, device = base + 16 + r, {"row": to}
             chosen = own[pl.ds(which * BLK, BLK), :]
             if masked:
@@ -129,20 +131,33 @@
         return copies
 
     loads[0].wait()
-    feat_copies = exchange(feat_v, snd_a, tab1, NB, a_ss, a_rs, False, 0, N_OFF)
+    feat_copies = exchange(feat_v, snd_a, tab1, NB, a_ss, a_rs, False, TURNS)
     loads[1].wait()
-    hist_copies = exchange(hist_v, snd_b, tab2, NB, b_ss, b_rs, False, 0, N_OFF)
+    hist_copies = exchange(hist_v, snd_b, tab2, NB, b_ss, b_rs, False, TURNS)
 
     zero_block = jnp.zeros((BLK, W), BF)
     for table in (tab1, tab2):
         table[blk(NB + c), :] = zero_block
         table[blk(NB + 16 + r), :] = zero_block
 
-    loads[2].wait()
+
+    def adj_load(i):
+        return pltpu.make_async_copy(
+            adj_h.at[rows(i * BLK * TPB, BLK * TPB)], adjr.at[i % RING], adj_sem.at[i % RING]
+        )
+
+    for i in range(RING):
+        adj_load(i).start()
 
     @pl.loop(0, NB)
     def _(i):
-        scr[...] = adjr[rows(i * BLK * TPB, BLK * TPB), :].astype(F32)
+        adj_load(i).wait()
+        scr[...] = adjr[i % RING].astype(F32)
+
+        @pl.when(i + RING < NB)
+        def _():
+            adj_load(i + RING).start()
+
         total = jnp.zeros((BLK, BLK), F32)
         for t in range(TPB):
             tile = scr[pl.ds(t, BLK, stride=TPB), :]
@@ -154,7 +169,7 @@
         d = deg[at, :]
         return v / jnp.concatenate([d] * (W // BLK), axis=1)
 
-    for n in range(3, 9):
+    for n in range(2, 8):
         loads[n].wait()
 
     @pl.loop(0, 8)
@@ -169,12 +184,12 @@
         @pl.loop(0, NB)
         def _(i):
             for jj in range(2):
-                strip_part = jnp.zeros((BLK, BLK), F32)
+                strip_part = jnp.zeros((BLK, BLK), BF)
                 for t in range(TPB):
-                    source = jnp.full((BLK, BLK), ts[i, t], jnp.int32)
-                    tile = adjd[blk(i), pl.ds(t * BLK, BLK)].astype(F32)
-                    strip_part += jnp.where(source == jp * 2 + jj, tile, 0.0)
-                strip[blk(i), pl.ds(jj * BLK, BLK)] = strip_part.astype(BF)
+                    source = jnp.full((BLK, BLK), ts[t, i], jnp.int32)
+                    hit = jnp.where(source == jp * 2 + jj, 1.0, 0.0).astype(BF)
+                    strip_part += hit * adjd[blk(i), pl.ds(t * BLK, BLK)]
+                strip[blk(i), pl.ds(jj * BLK, BLK)] = strip_part
 
         at = rows((jp % 2) * 256, 256)
         acc[jp // 2, at, :] += dot_tn(strip[...], bm[...])
@@ -185,7 +200,7 @@
             total = jnp.zeros((BLK, W), F32)
             for t in range(0, TPB, 2):
                 pair = jnp.concatenate(
-                    [table[pl.ds(ts[i, t + d] * BLK, BLK), :] for d in range(2)], axis=0
+                    [table[pl.ds(ts[t + d, i] * BLK, BLK), :] for d in range(2)], axis=0
                 )
                 total += dot(adjd[blk(i), pl.ds(t * BLK, 2 * BLK)], pair)
             out[blk(i), :] = divide(total, blk(i)).astype(BF)
@@ -210,12 +225,14 @@
         one.wait_send()
     fresh_copies = []
 
-    def send_fresh(part):
-        fresh_copies.extend(
-            exchange(hid_v, snd_a, fresh_h, 0, f_ss, f_rs, True, FRESH_CUTS[part], FRESH_CUTS[part + 1])
-        )
-
-    send_fresh(0)
+    def send_fresh(turns):
+        fresh_copies.extend(exchange(hid_v, snd_a, fresh_h, 0, f_ss, f_rs, True, turns))
+
+    def send_fresh_cols(part):
+        send_fresh([("col", n) for n in range(FRESH_CUTS[part], FRESH_CUTS[part + 1])])
+
+    send_fresh([("row", n) for n in range(ROWS_EARLY)])
+    send_fresh_cols(0)
 
     def grad_of(g, left, right):
         @pl.loop(0, 4)
@@ -223,11 +240,10 @@
             at = rows(q * BLK, BLK)
             acc[g, at, :] = dot_tn(left[:, at], right[...])
 
-    grad_of(0, feat_v, bp)
-    grad_of(1, fm, bp)
-    grad_of(2, hid_v, cot)
-
-    sems = iter(range(64))
+    sems = iter(range(96))
+    other = z * 2 + 1 - k
+    row_base = k * 256 + z * 64
+    reduce_copies = []
 
     def send(src, dst, device):
         n = next(sems)
@@ -236,19 +252,18 @@
             device_id=device, device_id_type=MESH,
         )
         one.start()
+        reduce_copies.append(one)
         return one
 
-    other = z * 2 + 1 - k
-    reduce_copies = []
+    def arrived(copies):
+        for one in copies:
+            one.wait_recv()
 
     def core_send(g, n):
         part = pl.ds(g, n)
-        one = send(acc.at[part, rows((1 - k) * 256, 256)], rv1.at[part], {"row": other})
-        reduce_copies.append(one)
-        return one
-
-    def z_send(g, n, core_copy):
-        core_copy.wait_recv()
+        return [send(acc.at[part, rows((1 - k) * 256, 256)], rv1.at[part], {"row": other})]
+
+    def z_send(g, n):
         for p in range(g, g + n):
             at = rows(k * 256, 256)
             both = acc[p, at, :] + rv1[p]
@@ -258,22 +273,71 @@
         copies = []
         for d in range(3):
             zt = (z + d + 1) % 4
-            copies.append(
-                send(s2.at[part, rows(zt * 64, 64)], rv2.at[d, part], {"row": zt * 2 + k})
-            )
-        reduce_copies.extend(copies)
+            copies.append(send(s2.at[part, rows(zt * 64, 64)], rv2.at[d, part], {"row": zt * 2 + k}))
         return copies
 
-    core_a = core_send(0, 3)
-    for one in hist_copies:
-        one.wait_recv()
-    z_a = z_send(0, 3, core_a)
-    send_fresh(1)
+    def xy_send(g, n):
+        for p in range(g, g + n):
+            total = acc[p, rows(row_base, 64), :]
+            for d in range(3):
+                total = total + rv2[d, p].astype(F32)
+            for d in range(16):
+                cut = total[(d // 4) * 16 : (d // 4) * 16 + 16, (d % 4) * BLK : (d % 4) * BLK + BLK]
+                h3[d, pl.ds(p * 16, 16), :] = cut
+                s3[d, pl.ds(p * 16, 16), :] = cut.astype(BF)
+        part = pl.ds(g * 16, n * 16)
+        copies = []
+        for m in range(len(COL_OFFS)):
+            to = col_of(m)
+            copies.append(send(s3.at[to, part], rv3.at[m, part], {"col": to}))
+        return copies
+
+    def xy_gather(g, n):
+        part = pl.ds(g * 16, n * 16)
+        total = h3[c, part, :]
+        for m in range(len(COL_OFFS)):
+            total = total + rv3[m, part, :].astype(F32)
+        g3[c, part, :] = total.astype(BF)
+        here = g3.at[c, part]
+        return [send(here, here, {"col": col_of(m)}) for m in range(len(COL_OFFS))]
+
+    def z_gather(g, n):
+        for p in range(g, g + n):
+            for d in range(16):
+                at = rows(row_base + (d // 4) * 16, 16)
+                gfin[p, at, pl.ds((d % 4) * BLK, BLK)] = g3[d, pl.ds(p * 16, 16), :]
+        here = gfin.at[pl.ds(g, n), rows(row_base, 64)]
+        return [send(here, here, {"row": ((z + d + 1) % 4) * 2 + k}) for d in range(3)]
+
+    def core_gather(g, n):
+        here = gfin.at[pl.ds(g, n), rows(k * 256, 256)]
+        return [send(here, here, {"row": other})]
+
+    z_a = []
+    grad_of(2, hid_v, cot)
+    core_2 = core_send(2, 1)
+    grad_of(0, feat_v, bp)
+    core_0 = core_send(0, 1)
+    arrived(core_2)
+    z_a += z_send(2, 1)
+    grad_of(1, fm, bp)
+    core_1 = core_send(1, 1)
+    arrived(core_0)
+    z_a += z_send(0, 1)
+    arrived(core_1)
+    z_a += z_send(1, 1)
+    send_fresh([("row", n) for n in range(ROWS_EARLY, len(ROW_OFFS))])
+
+    arrived(hist_copies)
     aggregate(tab2, sm)
+    arrived(z_a)
+    xy_a = xy_send(0, 3)
     grad_of(3, sm, cot)
     core_b = core_send(3, 1)
-
-    snd_b_done = [one.wait_send() for one in hist_copies]
+    send_fresh_cols(1)
+
+    for one in hist_copies:
+        one.wait_send()
     snd_b[pl.ds(0, BLK), :] = zero_block
     own_slots = [
         pltpu.make_async_copy(snd_b.at[pl.ds(0, BLK)], fresh_h.at[blk(c)], out_sem.at[0]),
@@ -282,7 +346,11 @@
     for one in own_slots:
         one.start()
 
-    z_b = z_send(3, 1, core_b)
+    arrived(core_b)
+    z_b = z_send(3, 1)
+    arrived(xy_a)
+    xy_a = xy_gather(0, 3)
+    send_fresh_cols(2)
 
     @pl.loop(0, 4)
     def _(m):
@@ -292,46 +360,21 @@
     emb_copy = pltpu.make_async_copy(bm, emb_h, out_sem.at[2])
     emb_copy.start()
 
-    for one in z_a + z_b:
-        one.wait_recv()
-    for p in range(4):
-        total = acc[p, rows(k * 256 + z * 64, 64), :]
-        for d in range(3):
-            total = total + rv2[d, p].astype(F32)
-        h3[p] = total
-        s3[p] = total.astype(BF)
-
-    def piece(to):
-        return (slice(None), rows((to // 4) * 16, 16), rows((to % 4) * BLK, BLK))
-
-    xy_copies = []
-    for n in range(len(COL_OFFS)):
-        to = col_of(n)
-        xy_copies.append(send(s3.at[piece(to)], rv3.at[n], {"col": to}))
-    reduce_copies.extend(xy_copies)
-    send_fresh(2)
-    mine = (slice(None), rows(x * 16, 16), rows(y * BLK, BLK))
-    final = h3[mine]
-    for one in xy_copies:
-        one.wait_recv()
-    for n in range(len(COL_OFFS)):
-        final = final + rv3[n].astype(F32)
-    here = (slice(None), rows(k * 256 + z * 64 + x * 16, 16), rows(y * BLK, BLK))
-    gfin[here] = final.astype(BF)
-
-    gather = [send(gfin.at[here], gfin.at[here], {"col": col_of(n)}) for n in range(len(COL_OFFS))]
-    for one in gather:
-        one.wait_recv()
-    reduce_copies.extend(gather)
-    strip_z = (slice(None), rows(k * 256 + z * 64, 64))
-    gather = [send(gfin.at[strip_z], gfin.at[strip_z], {"row": ((z + d + 1) % 4) * 2 + k}) for d in range(3)]
-    for one in gather:
-        one.wait_recv()
-    reduce_copies.extend(gather)
-    strip_k = (slice(None), rows(k * 256, 256))
-    one = send(gfin.at[strip_k], gfin.at[strip_k], {"row": other})
-    one.wait_recv()
-    reduce_copies.append(one)
+    arrived(z_b)
+    xy_b = xy_send(3, 1)
+    send_fresh_cols(3)
+    arrived(xy_a)
+    z_a = z_gather(0, 3)
+    arrived(xy_b)
+    xy_b = xy_gather(3, 1)
+    send_fresh_cols(4)
+    arrived(xy_b)
+    z_b = z_gather(3, 1)
+    arrived(z_a)
+    core_a = core_gather(0, 3)
+    arrived(z_b)
+    core_b = core_gather(3, 1)
+    arrived(core_a + core_b)
     grad_copy = pltpu.make_async_copy(gfin, grad_h, out_sem.at[3])
     grad_copy.start()
 
@@ -371,7 +414,7 @@
             vm((N_OFF * BLK, W), BF),
             vm((N_OFF * BLK, W), BF),
             vm((LOC, W), BF),
-            vm((LOC * TPB, BLK), BF),
+            vm((RING, BLK * TPB, BLK), BF),
             vm((LOC, TPB * BLK), BF),
             vm((BLK * TPB, BLK), F32),
             vm((LOC, BLK), F32),
@@ -379,27 +422,26 @@
             vm((LOC, W), BF),
             vm((LOC, W), BF),
             vm((4, W, W), F32),
-            vm((LOC, W), BF),
-            vm((LOC, W), BF),
             vm((LOC, 2 * BLK), BF),
             vm((4, 256, W), F32),
             vm((4, 256, W), BF),
             vm((3, 4, 64, W), BF),
-            vm((4, 64, W), BF),
-            vm((4, 64, W), F32),
-            vm((15, 4, 16, BLK), BF),
+            vm((16, 64, BLK), BF),
+            vm((16, 64, BLK), F32),
+            vm((15, 64, BLK), BF),
+            vm((16, 64, BLK), BF),
             vm((4, W, W), BF),
-            dma((9,)), dma((4,)),
+            dma((8,)), dma((RING,)), dma((4,)),
             dma((N_OFF,)), dma((N_OFF,)), dma((N_OFF,)), dma((N_OFF,)), dma((N_OFF,)), dma((N_OFF,)),
-            dma((42,)), dma((42,)),
+            dma((96,)), dma((96,)),
         ],
         compiler_params=pltpu.CompilerParams(
-            collective_id=0, has_side_effects=True, vmem_limit_bytes=61 * 2**20
+            collective_id=0, has_side_effects=True, vmem_limit_bytes=56 * 2**20
         ),
         cost_estimate=pl.CostEstimate(flops=18 * 10**9, bytes_accessed=24 * 2**20, transcendentals=2**20),
     )(
-        features, history, cotangent, adjacency.reshape(LOC * TPB, BLK), tile_source,
-        col_sends, col_counts, row_sends, row_counts,
+        features, history, cotangent, adjacency.reshape(LOC * TPB, BLK), tile_source.T,
+        col_sends.reshape(1, -1), col_counts, row_sends.reshape(1, -1), row_counts,
         first_self, first_neigh, second_self, second_neigh,
     )
     return emb, fresh, *(grads[n].astype(F32) for n in range(4))

time: 125 us -> 114 us (0.912)
  Pallas kernels: 112 us -> 105 us
  local copies, waits for them, and re-layouts: 8.32 us -> 4.31 us
    pallas_call x1, Pallas kernels: 112 us -> 105 us  [body(): pl.pallas_call(kernel, out_shape=(jax.ShapeDtypeStruct((LOC, W), BF), jax...]
    unnamed x9 -> x6, local copies, waits for them, and re-layouts: 8.32 us -> 4.31 us
where the time goes in v2:
time: 114 us
  Pallas kernels  105 us (92%)
  local copies, waits for them, and re-layouts  4.31 us (4%)
  other arithmetic  3.9 us (3%)
    pallas_call x1, Pallas kernels, body(): pl.pallas_call(kernel, out_shape=(jax.ShapeDtypeStruct((LOC, W), BF), jax...  105 us
    unnamed x6, local copies, waits for them, and re-layouts  4.31 us
    convert_element_type x1, other arithmetic, body(): return (emb, fresh, *(grads[n].astype(F32) for n in range(4)))  3.9 us

profile of v2, /device:TPU:1, one launch (start us, length us, event | category | flops | bytes accessed | tf_op | source)
XLA Modules:
  0.0 114.0 jit_solution(7629877528546313114)
XLA Ops:
  0.6 105.1 %shard_map.172 = (bf16[2048,512]{1,0:T(8,128)(2,1)}, bf16[3072,512]{1,0:T(8,128)(2,1)}, bf16[4,512,512]{2,1,0:T(8,128)(2,1)}) custom-call(bf16[2048,512]{1,0:T(8,128)(2,1)} %feat_h.1, bf16[2048,512]{1,0:T(8,128)(2,1)} %hist_h.1, bf16[2048,512]{1,0:T(8,128)(2,1)} %cot_h.1, bf16[16384,128]{1,0:T(8,128)(2,1)} %bitcast.16, s32[8,16]{1,0:T(8,128)} %bitcast.17, ...), custom_call_target="tpu_custom_call" | custom-call | flops 17999998976 | bytes 25165824 | tf_op jit(solution)/shard_map/pallas_call | solution.py:399
  105.7 0.0 copy-start.1
  105.7 3.9 %bitcast_convert_fusion = (f32[512,512]{1,0:T(8,128)}, f32[512,512]{1,0:T(8,128)}, f32[512,512]{1,0:T(8,128)}, f32[512,512]{1,0:T(8,128)}) fusion(bf16[4,512,512]{2,1,0:T(8,128)(2,1)} %get-tuple-element.11), kind=kLoop, calls=%fused_computation | loop fusion | flops 1048576 | bytes 6291456 | tf_op jit(solution)/shard_map/convert_element_type | solution.py:447
  109.6 0.0 copy-done.1
  109.7 0.0 copy-start
  109.7 1.3 %copy.21 = bf16[2048,512]{1,0:T(8,128)(2,1)} copy(bf16[2048,512]{1,0:T(8,128)(2,1)S(1)} %copy-done.1) | data formatting | bytes 4194304
  111.0 1.3 %copy-done = bf16[3072,512]{1,0:T(8,128)(2,1)S(1)} copy-done((bf16[3072,512]{1,0:T(8,128)(2,1)S(1)}, bf16[3072,512]{1,0:T(8,128)(2,1)}, u32[]{:S(2)}) %copy-start) | copy-done | bytes 3145752
  112.3 1.7 %copy.22 = bf16[3072,512]{1,0:T(8,128)(2,1)} copy(bf16[3072,512]{1,0:T(8,128)(2,1)S(1)} %copy-done) | data formatting | bytes 6291456
Async XLA Ops:
  105.7 3.9 %copy-start.1 = (bf16[2048,512]{1,0:T(8,128)(2,1)S(1)}, bf16[2048,512]{1,0:T(8,128)(2,1)}, u32[]{:S(2)}) copy-start(bf16[2048,512]{1,0:T(8,128)(2,1)} %get-tuple-element.22) | copy-start | bytes 6291460
  109.7 2.6 %copy-start = (bf16[3072,512]{1,0:T(8,128)(2,1)S(1)}, bf16[3072,512]{1,0:T(8,128)(2,1)}, u32[]{:S(2)}) copy-start(bf16[3072,512]{1,0:T(8,128)(2,1)} %get-tuple-element.23) | copy-start | bytes 9437188

commit v3 on v2

--- a/solution.py
+++ b/solution.py
@@ -399,12 +399,12 @@
     emb, fresh, grads = pl.pallas_call(
         kernel,
         out_shape=(
-            jax.ShapeDtypeStruct((LOC, W), BF),
-            jax.ShapeDtypeStruct((24 * BLK, W), BF),
-            jax.ShapeDtypeStruct((4, W, W), BF),
+            pltpu.VMEM((LOC, W), BF),
+            pltpu.VMEM((24 * BLK, W), BF),
+            pltpu.VMEM((4, W, W), BF),
         ),
         in_specs=[anyspace] * 4 + [smem] * 5 + [anyspace] * 4,
-        out_specs=(anyspace,) * 3,
+        out_specs=(pl.BlockSpec(memory_space=pl.ANY),) * 3,
         scratch_shapes=[
             vm((40 * BLK, W), BF),
             vm((40 * BLK, W), BF),
@@ -436,7 +436,7 @@
             dma((96,)), dma((96,)),
         ],
         compiler_params=pltpu.CompilerParams(
-            collective_id=0, has_side_effects=True, vmem_limit_bytes=56 * 2**20
+            collective_id=0, has_side_effects=True, vmem_limit_bytes=54 * 2**20
         ),
         cost_estimate=pl.CostEstimate(flops=18 * 10**9, bytes_accessed=24 * 2**20, transcendentals=2**20),
     )(

time: 114 us -> 110 us (0.965)
  other arithmetic: 3.9 us -> 2.24 us
  local copies, waits for them, and re-layouts: 4.31 us -> 2.99 us
    convert_element_type x1, other arithmetic: 3.9 us -> 2.24 us  [body(): return (emb, fresh, *(grads[n].astype(F32) for n in range(4)))]
    unnamed x6 -> x2, local copies, waits for them, and re-layouts: 4.31 us -> 2.99 us
where the time goes in v3:
time: 110 us
  Pallas kernels  104 us (95%)
  local copies, waits for them, and re-layouts  2.99 us (3%)
  other arithmetic  2.24 us (2%)
    pallas_call x1, Pallas kernels, body(): pl.pallas_call(kernel, out_shape=(pltpu.VMEM((LOC, W), BF), pltpu.VMEM((2...  104 us
    unnamed x2, local copies, waits for them, and re-layouts  2.99 us
    convert_element_type x1, other arithmetic, body(): return (emb, fresh, *(grads[n].astype(F32) for n in range(4)))  2.24 us

profile of v3, /device:TPU:1, one launch (start us, length us, event | category | flops | bytes accessed | tf_op | source)
XLA Modules:
  0.0 110.1 jit_solution(11616574478254301189)
XLA Ops:
  0.6 104.3 %shard_map.172 = (bf16[2048,512]{1,0:T(8,128)(2,1)S(1)}, bf16[3072,512]{1,0:T(8,128)(2,1)S(1)}, bf16[4,512,512]{2,1,0:T(8,128)(2,1)S(1)}) custom-call(bf16[2048,512]{1,0:T(8,128)(2,1)} %feat_h.1, bf16[2048,512]{1,0:T(8,128)(2,1)} %hist_h.1, bf16[2048,512]{1,0:T(8,128)(2,1)} %cot_h.1, bf16[16384,128]{1,0:T(8,128)(2,1)} %bitcast.16, s32[8,16]{1,0:T(8,128)} %bitcast.17, ...), custom_call_target="tpu_custom_call" | custom-call | flops 17999998976 | bytes 25165824 | tf_op jit(solution)/shard_map/pallas_call | solution.py:399
  104.9 1.3 %copy.21 = bf16[2048,512]{1,0:T(8,128)(2,1)} copy(bf16[2048,512]{1,0:T(8,128)(2,1)S(1)} %get-tuple-element.16) | data formatting | bytes 4194304
  106.2 1.7 %copy.22 = bf16[3072,512]{1,0:T(8,128)(2,1)} copy(bf16[3072,512]{1,0:T(8,128)(2,1)S(1)} %get-tuple-element.17) | data formatting | bytes 6291456
  107.9 2.2 %bitcast_convert_fusion = (f32[512,512]{1,0:T(8,128)}, f32[512,512]{1,0:T(8,128)}, f32[512,512]{1,0:T(8,128)}, f32[512,512]{1,0:T(8,128)}) fusion(bf16[4,512,512]{2,1,0:T(8,128)(2,1)S(1)} %get-tuple-element.11), kind=kLoop, calls=%fused_computation | loop fusion | flops 1048576 | bytes 6291456 | tf_op jit(solution)/shard_map/convert_element_type | solution.py:447

commit v4 on v3

--- a/solution.py
+++ b/solution.py
@@ -31,7 +31,7 @@
     TURNS.append(("col", _n))
     if _n % 2 == 0 and _n // 2 < len(ROW_OFFS):
         TURNS.append(("row", _n // 2))
-FRESH_CUTS = (0, 5, 8, 11, 13, 15)
+FRESH_CUTS = (0, 5, 6, 6, 7, 15)
 
 
 def dot(a, b):
@@ -374,9 +374,12 @@
     core_a = core_gather(0, 3)
     arrived(z_b)
     core_b = core_gather(3, 1)
-    arrived(core_a + core_b)
-    grad_copy = pltpu.make_async_copy(gfin, grad_h, out_sem.at[3])
-    grad_copy.start()
+    grad_copies = []
+    for g, n, last in ((0, 3, core_a), (3, 1, core_b)):
+        arrived(last)
+        part = pl.ds(g, n)
+        grad_copies.append(pltpu.make_async_copy(gfin.at[part], grad_h.at[part], out_sem.at[3 + g // 3]))
+        grad_copies[-1].start()
 
     for one in fresh_copies:
         one.wait_recv()
@@ -385,7 +388,8 @@
     for one in own_slots:
         one.wait()
     emb_copy.wait()
-    grad_copy.wait()
+    for one in grad_copies:
+        one.wait()
 
 
 def body(
@@ -431,7 +435,7 @@
             vm((15, 64, BLK), BF),
             vm((16, 64, BLK), BF),
             vm((4, W, W), BF),
-            dma((8,)), dma((RING,)), dma((4,)),
+            dma((8,)), dma((RING,)), dma((5,)),
             dma((N_OFF,)), dma((N_OFF,)), dma((N_OFF,)), dma((N_OFF,)), dma((N_OFF,)), dma((N_OFF,)),
             dma((96,)), dma((96,)),
         ],

time: 110 us -> 108 us (0.982); the launches traced: 110 us -> 107 us
  Pallas kernels: 104 us -> 101 us
    pallas_call x1, Pallas kernels: 104 us -> 101 us  [body(): pl.pallas_call(kernel, out_shape=(pltpu.VMEM((LOC, W), BF), pltpu.VMEM((2...]
where the time goes in v4:
time: 108 us; the launch traced here: 107 us
  Pallas kernels  101 us (94%)
  local copies, waits for them, and re-layouts  2.99 us (3%)
  other arithmetic  2.24 us (2%)
    pallas_call x1, Pallas kernels, body(): pl.pallas_call(kernel, out_shape=(pltpu.VMEM((LOC, W), BF), pltpu.VMEM((2...  101 us
    unnamed x2, local copies, waits for them, and re-layouts  2.99 us
    convert_element_type x1, other arithmetic, body(): return (emb, fresh, *(grads[n].astype(F32) for n in range(4)))  2.24 us

profile of v4, /device:TPU:1, one launch (start us, length us, event | category | flops | bytes accessed | tf_op | source)
XLA Modules:
  0.0 107.0 jit_solution(7350205601202584106)
XLA Ops:
  0.6 101.1 %shard_map.172 = (bf16[2048,512]{1,0:T(8,128)(2,1)S(1)}, bf16[3072,512]{1,0:T(8,128)(2,1)S(1)}, bf16[4,512,512]{2,1,0:T(8,128)(2,1)S(1)}) custom-call(bf16[2048,512]{1,0:T(8,128)(2,1)} %feat_h.1, bf16[2048,512]{1,0:T(8,128)(2,1)} %hist_h.1, bf16[2048,512]{1,0:T(8,128)(2,1)} %cot_h.1, bf16[16384,128]{1,0:T(8,128)(2,1)} %bitcast.16, s32[8,16]{1,0:T(8,128)} %bitcast.17, ...), custom_call_target="tpu_custom_call" | custom-call | flops 17999998976 | bytes 25165824 | tf_op jit(solution)/shard_map/pallas_call | solution.py:403
  101.7 1.3 %copy.21 = bf16[2048,512]{1,0:T(8,128)(2,1)} copy(bf16[2048,512]{1,0:T(8,128)(2,1)S(1)} %get-tuple-element.16) | data formatting | bytes 4194304
  103.1 1.7 %copy.22 = bf16[3072,512]{1,0:T(8,128)(2,1)} copy(bf16[3072,512]{1,0:T(8,128)(2,1)S(1)} %get-tuple-element.17) | data formatting | bytes 6291456
  104.7 2.2 %bitcast_convert_fusion = (f32[512,512]{1,0:T(8,128)}, f32[512,512]{1,0:T(8,128)}, f32[512,512]{1,0:T(8,128)}, f32[512,512]{1,0:T(8,128)}) fusion(bf16[4,512,512]{2,1,0:T(8,128)(2,1)S(1)} %get-tuple-element.11), kind=kLoop, calls=%fused_computation | loop fusion | flops 1048576 | bytes 6291456 | tf_op jit(solution)/shard_map/convert_element_type | solution.py:451
